TPU v7x, 512 devices: a whole 4x4x16 slice. The times are simulated.
512 devices in a mesh: dp: 8 (over y, core), node: 64 (over z, x).
Axes of the slice: x: 4, y: 4, z: 16, core: 2. Of those that a mesh axis runs over, the one named last changes fastest.
Arguments:
- leaf_logp: float32 [128, 32, 1024], P('node', None, 'dp'), may hold values from -108 to 0, as said below
- weights: bfloat16 [128, 32, 1024], P('node'), may hold values from 0.0099487305 to 1
- upper_flows: float32 [128, 32, 1024], P('node', None, 'dp'), may hold values from 0.01 to 1
- leaf_asks: int32 [64, 64], P('node'), may hold values from 0 to 1
- prod_asks: int32 [64, 64], P('node'), may hold values from 0 to 1
- prod_child: int32 [128, 8], P('node'), may hold values from 0 to 63
- prod_valid: int32 [128, 8], P('node'), may hold values 0 or 1
- sum_child: int32 [128, 32], P('node'), may hold values from 0 to 63
- sum_valid: int32 [128, 32], P('node'), may hold values from 0 to 1, as said below
Outputs:
- sum_loglik: float32 [128, 32, 1024], P('node', None, 'dp')
- weight_flows: float32 [128, 32, 1024], P('node', None, 'dp')
- prod_flows: float32 [128, 32, 1024], P('node', None, 'dp')
Inputs may be any that keep to these rules, and one draw needn't show every extreme that they name: `leaf_logp`: log-probabilities, so no entry is positive. `leaf_asks`: entry (d, o) is which of owner o's 2 blocks device d reads. `prod_asks`: entry (d, o) is which of owner o's 2 blocks device d reads. `sum_valid`: the first child slot of every sum block is valid.
All inputs are finite; a program needn't handle non-finite values. No bound on the sum of `prod_valid` on one device may be relied on, other than what follows from the above.
Results may differ from a plain program's by a relative error of at most 0.0022.
Values sent between devices are 32-bit elements; how exact they have to be, the bound alone decides.
A program may use at most 64 MiB of HBM per device.

v0:
```python
import jax
import jax.numpy as jnp
from jax import lax
from jax.sharding import PartitionSpec as P


def local(
    leaf_logp,
    weights,
    upper_flows,
    leaf_asks,
    prod_asks,
    prod_child,
    prod_valid,
    sum_child,
    sum_valid,
):
    block_count, node_width, tok_count = leaf_logp.shape
    owners = lax.axis_size("node")
    slot_iota = jnp.arange(owners, dtype=jnp.int32)
    block_iota = jnp.arange(block_count, dtype=jnp.int32)
    exact = lax.Precision.HIGHEST
    asked = (
        lax.all_to_all(
            leaf_asks.reshape(owners, 1), "node", split_axis=0, concat_axis=0, tiled=True
        ),
        lax.all_to_all(
            prod_asks.reshape(owners, 1), "node", split_axis=0, concat_axis=0, tiled=True
        ),
    )
    ask_rows = (leaf_asks[0], prod_asks[0])

    def fetch_blocks(layer_vals, which_ask):
        whole_layer = lax.all_gather(layer_vals, "node", axis=0, tiled=True)
        return whole_layer[slot_iota * block_count + ask_rows[which_ask]]

    leaf_slots = fetch_blocks(leaf_logp, 0)
    mix_count = jnp.sum(
        (prod_child[:, :, None] == slot_iota[None, None, :]) * prod_valid[:, :, None], axis=1
    ).astype(jnp.float32)
    products = jnp.einsum("bo,okt->bkt", mix_count, leaf_slots, precision=exact)
    prod_slots = fetch_blocks(products, 1)
    picked = prod_slots[sum_child]
    is_valid = (sum_valid > 0)[:, :, None, None]
    col_max = jnp.max(jnp.where(is_valid, picked, -jnp.inf), axis=(1, 2))
    scaled = jnp.where(is_valid, jnp.exp(picked - col_max[:, None, None, :]), 0.0).astype(
        jnp.bfloat16
    )
    edges = picked.shape[1]
    flat_rows = scaled.reshape(block_count, edges * node_width, tok_count)
    totals = jnp.einsum("bkj,bjt->bkt", weights, flat_rows, preferred_element_type=jnp.float32)
    sum_loglik = jnp.log(totals) + col_max[:, None, :]
    ratios = (upper_flows / totals).astype(jnp.bfloat16)
    partial_counts = jnp.einsum(
        "bkt,bjt->bkj", ratios, flat_rows, preferred_element_type=jnp.float32
    )
    summed_counts = lax.psum_scatter(partial_counts, "dp", scatter_dimension=2, tiled=True)
    share_cols = summed_counts.shape[2]
    col_start = lax.axis_index("dp") * share_cols
    weight_cols = lax.dynamic_slice_in_dim(weights, col_start, share_cols, 2).astype(jnp.float32)
    weight_flows = weight_cols * summed_counts / (tok_count * lax.axis_size("dp"))
    spread_back = jnp.einsum("bkj,bkt->bjt", weights, ratios, preferred_element_type=jnp.float32)
    child_flows = (flat_rows.astype(jnp.float32) * spread_back).reshape(
        block_count, edges, node_width, tok_count
    )
    routing = (sum_child[:, :, None] == slot_iota[None, None, :]).astype(jnp.float32)
    slot_flows = jnp.einsum("beo,bekt->okt", routing, child_flows, precision=exact)
    returned = lax.all_to_all(slot_flows, "node", split_axis=0, concat_axis=0, tiled=True)
    pick_block = (asked[1][:, 0][:, None] == block_iota[None, :]).astype(jnp.float32)
    prod_flows = jnp.einsum("cb,ckt->bkt", pick_block, returned, precision=exact)
    return (sum_loglik, weight_flows, prod_flows)


def solution(mesh):
    in_specs = (
        P("node", None, "dp"),
        P("node", None, None),
        P("node", None, "dp"),
        P("node", None),
        P("node", None),
        P("node", None),
        P("node", None),
        P("node", None),
        P("node", None),
    )
    out_specs = (P("node", None, "dp"), P("node", None, "dp"), P("node", None, "dp"))
    return jax.shard_map(local, mesh=mesh, in_specs=in_specs, out_specs=out_specs, check_vma=False)
```

profile of v0, /device:TPU:2, one launch (start us, length us, event | category | flops | bytes accessed | tf_op | source)
XLA Modules:
  0.0 369.7 jit_solution(18280250931427675096)
XLA Ops:
  7.2 0.7 all-gather.3.cloned.1.call-update
  8.0 0.7 fusion.14
  8.6 0.8 select_reduce_fusion.1
  9.4 145.9 %all-gather.3.cloned.1.call-done = f32[128,32,128]{2,1,0:T(8,128)} async-done(((f32[2,32,128]{2,1,0:T(8,128)}), f32[128,32,128]{2,1,0:T(8,128)}) %all-gather.3.cloned.1.call-update) | async-done | bytes 2097168 | tf_op jit(solution)/shard_map/all_gather | solution.py:34
  155.3 2.2 gather_fusion
  157.5 1.2 fusion.4
  158.7 0.6 copy.46
  159.3 0.7 copy.50
  160.0 11.5 %all-to-all-start = ((s32[64,1,1]{2,1,0:T(1,128)}), s32[64,1,1]{2,1,0:T(1,128)S(1)}, u32[]{:S(2)}, u32[]{:S(2)}) async-start(s32[64,1,1]{2,1,0:T(1,128)} %copy.50), calls=%async_computation.1 | async-start | bytes 65536 | tf_op jit(solution)/shard_map/all_to_all | solution.py:27
  171.5 0.1 reshape.88
  171.6 0.1 broadcast_in_dim.38
  171.7 0.1 broadcast_in_dim.39
  171.9 124.6 %all-gather.5.cloned.1.call-done = f32[128,32,128]{2,1,0:T(8,128)} async-done(((f32[2,32,128]{2,1,0:T(8,128)}), f32[128,32,128]{2,1,0:T(8,128)}) %all-gather.5.cloned.1.call-update) | async-done | bytes 2097168 | tf_op jit(solution)/shard_map/all_gather | solution.py:34
  296.4 2.2 gather_fusion.1
  298.6 0.6 gather_fusion.2
  299.3 0.2 select_reduce_fusion
  299.5 0.3 copy.47
  299.8 0.2 select_convert_fusion
  300.0 0.3 copy-done
  300.4 0.9 divide_convert_fusion
  301.3 0.3 fusion
  301.6 0.3 copy.51
  302.0 1.3 convolution_bitcast_fusion
  303.3 1.6 copy.53
  304.9 11.5 %all-to-all-start.1 = ((f32[64,32,128]{2,1,0:T(8,128)}), f32[64,32,128]{2,1,0:T(8,128)S(1)}, u32[]{:S(2)}, u32[]{:S(2)}) async-start(f32[64,32,128]{2,1,0:T(8,128)} %copy.53), calls=%async_computation.2 | async-start | bytes 2097152 | tf_op jit(solution)/shard_map/all_to_all | solution.py:68
  316.4 0.9 fusion.17
  317.4 1.2 reduce
  318.6 41.0 %reduce-scatter.2.cloned.1.call-done = f32[2,32,128]{2,1,0:T(8,128)} async-done(((f32[2,32,1024]{2,1,0:T(8,128)}), f32[2,32,128]{2,1,0:T(8,128)}) %reduce-scatter.2.cloned.1.call-update) | async-done | bytes 32784 | tf_op jit(solution)/shard_map/reduce_scatter | solution.py:57
  359.5 1.4 multiply_multiply_fusion
  360.9 0.5 all-to-all-done.1
  361.5 1.0 fusion.1
  362.5 0.6 copy.55
  (21 shorter events, 0.2 us)
Async XLA Ops:
  7.2 152.2 %copy-start.3 = (s32[1,64]{1,0:T(1,128)S(1)}, s32[1,64]{1,0:T(1,128)}, u32[]{:S(2)}) copy-start(s32[1,64]{1,0:T(1,128)} %param.13) | copy-start | bytes 772
  7.2 164.4 %copy-start.2 = (s32[2,32]{1,0:T(2,128)S(1)}, s32[2,32]{1,0:T(2,128)}, u32[]{:S(2)}) copy-start(s32[2,32]{1,0:T(2,128)} %param.16) | copy-start | bytes 772
  7.2 164.4 %copy-start.4 = (s32[2,32]{1,0:T(2,128)S(1)}, s32[2,32]{1,0:T(2,128)}, u32[]{:S(2)}) copy-start(s32[2,32]{1,0:T(2,128)} %param.17) | copy-start | bytes 772
  7.2 148.1 %all-gather.3.cloned.1.call-start = ((), (), s32[]{:S(2)}) async-start(), calls=%async_computation.3 | async-start | bytes 2129920 | tf_op jit(solution)/shard_map/all_gather | solution.py:34
  7.9 288.5 %all-gather.5.cloned.1.call-start = ((), (), s32[]{:S(2)}) async-start(), calls=%async_computation.4 | async-start | bytes 2129920 | tf_op jit(solution)/shard_map/all_gather | solution.py:34
  160.0 144.8 %all-to-all-start = ((s32[64,1,1]{2,1,0:T(1,128)}), s32[64,1,1]{2,1,0:T(1,128)S(1)}, u32[]{:S(2)}, u32[]{:S(2)}) async-start(s32[64,1,1]{2,1,0:T(1,128)} %copy.50), calls=%async_computation.1 | async-start | bytes 65536 | tf_op jit(solution)/shard_map/all_to_all | solution.py:27
  299.5 0.9 copy-start
  299.5 0.9 copy-start.1
  304.9 56.6 %all-to-all-start.1 = ((f32[64,32,128]{2,1,0:T(8,128)}), f32[64,32,128]{2,1,0:T(8,128)S(1)}, u32[]{:S(2)}, u32[]{:S(2)}) async-start(f32[64,32,128]{2,1,0:T(8,128)} %copy.53), calls=%async_computation.2 | async-start | bytes 2097152 | tf_op jit(solution)/shard_map/all_to_all | solution.py:68
  316.4 43.2 %reduce-scatter.2.cloned.1.call-start = ((), (), s32[]{:S(2)}) async-start(), calls=%async_computation.5 | async-start | bytes 294912 | tf_op jit(solution)/shard_map/reduce_scatter | solution.py:57
Sparse Core Ops, SparseCore 0:
  11.0 144.2 all-gather.2
  159.4 136.9 all-gather.4
  320.0 39.4 reduce-scatter.1
where the time goes:
time: 370 us
  waiting for transfers between devices  313 us (85%)
  starting transfers between devices  23.1 us (6%)
  between operations  13.9 us (4%)
  local copies, waits for them, and re-layouts  9.82 us (3%)
  matrix products  5.71 us (2%)
  other arithmetic  4.49 us (1%)
    all_gather x2, waiting for transfers between devices, fetch_blocks(): whole_layer = lax.all_gather(layer_vals, 'node', axis=0, tiled=True)  270 us
    reduce_scatter x1, waiting for transfers between devices, local(): lax.psum_scatter(partial_counts, 'dp', scatter_dimension=2, tiled=True)  41 us
    all_to_all x1, starting transfers between devices, local(): lax.all_to_all(prod_asks.reshape(owners, 1), 'node', split_axis=0, concat...  11.5 us
    all_to_all x1, starting transfers between devices, local(): lax.all_to_all(slot_flows, 'node', split_axis=0, concat_axis=0, tiled=True)  11.5 us
  transfers between devices with their start and end apart: 5, of which 4 were waited for; matrix products, arithmetic and copies ran while one was open for 4% of the time, Pallas kernels for 0%

commit v1 on v0

--- a/solution.py
+++ b/solution.py
@@ -31,7 +31,9 @@
     ask_rows = (leaf_asks[0], prod_asks[0])
 
     def fetch_blocks(layer_vals, which_ask):
-        whole_layer = lax.all_gather(layer_vals, "node", axis=0, tiled=True)
+        whole_layer = jnp.concatenate(
+            lax.all_to_all(jnp.stack([layer_vals] * lax.axis_size("node")), "node", 0, 0), axis=0
+        )
         return whole_layer[slot_iota * block_count + ask_rows[which_ask]]
 
     leaf_slots = fetch_blocks(leaf_logp, 0)

time: 370 us -> 328 us (0.89)
  the two profiles are of different devices: /device:TPU:2 before, /device:TPU:24 now
where the time goes in v1:
time: 328 us
  waiting for transfers between devices  257 us (78%)
  starting transfers between devices  38 us (12%)
  between operations  14.2 us (4%)
  local copies, waits for them, and re-layouts  10 us (3%)
  matrix products  5.71 us (2%)
    all_to_all x2, waiting for transfers between devices, fetch_blocks(): lax.all_to_all(jnp.stack([layer_vals] * lax.axis_size('node')), 'node', 0...  199 us
    reduce_scatter x1, waiting for transfers between devices, local(): lax.psum_scatter(partial_counts, 'dp', scatter_dimension=2, tiled=True)  37.9 us
    all_to_all x2, starting transfers between devices, fetch_blocks(): lax.all_to_all(jnp.stack([layer_vals] * lax.axis_size('node')), 'node', 0...  24.7 us
    all_to_all x1, waiting for transfers between devices, local(): lax.all_to_all(slot_flows, 'node', split_axis=0, concat_axis=0, tiled=True)  12.4 us
    all_to_all x1, waiting for transfers between devices, local(): lax.all_to_all(prod_asks.reshape(owners, 1), 'node', split_axis=0, concat...  7.68 us
    all_to_all x1, starting transfers between devices, local(): lax.all_to_all(slot_flows, 'node', split_axis=0, concat_axis=0, tiled=True)  7.42 us
  transfers between devices with their start and end apart: 5, of which 5 were waited for; matrix products, arithmetic and copies ran while one was open for 3% of the time, Pallas kernels for 0%

profile of v1, /device:TPU:24, one launch (start us, length us, event | category | flops | bytes accessed | tf_op | source)
XLA Modules:
  0.0 327.8 jit_solution(11461770835301077281)
XLA Ops:
  7.2 2.4 stack.4
  9.5 18.7 %all-to-all-start = ((f32[64,2,32,128]{3,2,1,0:T(8,128)}), f32[64,2,32,128]{3,2,1,0:T(8,128)S(1)}, u32[]{:S(2)}, u32[]{:S(2)}) async-start(f32[64,2,32,128]{3,2,1,0:T(8,128)} %stack.4), calls=%async_computation | async-start | bytes 4194304 | tf_op jit(solution)/shard_map/all_to_all | solution.py:35
  28.3 0.1 select_reduce_fusion.1
  28.4 100.1 %all-to-all-done = f32[64,2,32,128]{3,2,1,0:T(8,128)S(1)} async-done(((f32[64,2,32,128]{3,2,1,0:T(8,128)}), f32[64,2,32,128]{3,2,1,0:T(8,128)S(1)}, u32[]{:S(2)}, u32[]{:S(2)}) %all-to-all-start) | async-done | bytes 2097184 | tf_op jit(solution)/shard_map/all_to_all | solution.py:35
  128.5 0.6 gather_fusion
  129.1 1.2 fusion.4
  130.3 1.6 stack.5
  131.9 6.0 %all-to-all-start.1 = ((f32[64,2,32,128]{3,2,1,0:T(8,128)}), f32[64,2,32,128]{3,2,1,0:T(8,128)S(1)}, u32[]{:S(2)}, u32[]{:S(2)}) async-start(f32[64,2,32,128]{3,2,1,0:T(8,128)} %stack.5), calls=%async_computation.1 | async-start | bytes 4194304 | tf_op jit(solution)/shard_map/all_to_all | solution.py:35
  138.1 0.1 broadcast_in_dim.39
  138.2 0.7 copy.50
  138.9 98.7 %all-to-all-done.1 = f32[64,2,32,128]{3,2,1,0:T(8,128)S(1)} async-done(((f32[64,2,32,128]{3,2,1,0:T(8,128)}), f32[64,2,32,128]{3,2,1,0:T(8,128)S(1)}, u32[]{:S(2)}, u32[]{:S(2)}) %all-to-all-start.1) | async-done | bytes 2097184 | tf_op jit(solution)/shard_map/all_to_all | solution.py:35
  237.6 5.8 %all-to-all-start.2 = ((s32[64,1,1]{2,1,0:T(1,128)}), s32[64,1,1]{2,1,0:T(1,128)S(1)}, u32[]{:S(2)}, u32[]{:S(2)}) async-start(s32[64,1,1]{2,1,0:T(1,128)} %copy.50), calls=%async_computation.3 | async-start | bytes 65536 | tf_op jit(solution)/shard_map/all_to_all | solution.py:27
  243.4 0.6 gather_fusion.1
  244.1 0.6 gather_fusion.2
  244.7 0.2 select_reduce_fusion
  244.9 0.3 copy.47
  245.3 0.2 select_convert_fusion
  245.5 0.3 copy-done
  245.8 0.9 divide_convert_fusion
  246.7 0.3 fusion
  247.1 0.3 copy.51
  247.4 1.3 convolution_bitcast_fusion
  248.8 1.6 copy.53
  250.3 7.7 %all-to-all-done.2 = s32[64,1,1]{2,1,0:T(1,128)S(1)} async-done(((s32[64,1,1]{2,1,0:T(1,128)}), s32[64,1,1]{2,1,0:T(1,128)S(1)}, u32[]{:S(2)}, u32[]{:S(2)}) %all-to-all-start.2) | async-done | bytes 288 | tf_op jit(solution)/shard_map/all_to_all | solution.py:27
  258.0 7.4 %all-to-all-start.3 = ((f32[64,32,128]{2,1,0:T(8,128)}), f32[64,32,128]{2,1,0:T(8,128)S(1)}, u32[]{:S(2)}, u32[]{:S(2)}) async-start(f32[64,32,128]{2,1,0:T(8,128)} %copy.53), calls=%async_computation.4 | async-start | bytes 2097152 | tf_op jit(solution)/shard_map/all_to_all | solution.py:70
  265.5 0.9 fusion.17
  266.4 1.2 reduce
  267.7 37.9 %reduce-scatter.2.cloned.1.call-done = f32[2,32,128]{2,1,0:T(8,128)} async-done(((f32[2,32,1024]{2,1,0:T(8,128)}), f32[2,32,128]{2,1,0:T(8,128)}) %reduce-scatter.2.cloned.1.call-update) | async-done | bytes 32784 | tf_op jit(solution)/shard_map/reduce_scatter | solution.py:59
  305.6 1.4 multiply_multiply_fusion
  307.0 12.4 %all-to-all-done.3 = f32[64,32,128]{2,1,0:T(8,128)S(1)} async-done(((f32[64,32,128]{2,1,0:T(8,128)}), f32[64,32,128]{2,1,0:T(8,128)S(1)}, u32[]{:S(2)}, u32[]{:S(2)}) %all-to-all-start.3) | async-done | bytes 1048608 | tf_op jit(solution)/shard_map/all_to_all | solution.py:70
  319.3 1.0 fusion.1
  320.4 0.6 copy.55
  (27 shorter events, 0.3 us)
Async XLA Ops:
  9.5 18.7 %copy-start.7 = (s32[1,64]{1,0:T(1,128)S(1)}, s32[1,64]{1,0:T(1,128)}, u32[]{:S(2)}) copy-start(s32[1,64]{1,0:T(1,128)} %param.12) | copy-start | bytes 772
  9.5 18.7 %copy-start.3 = (s32[2,8]{1,0:T(2,128)S(1)}, s32[2,8]{1,0:T(2,128)}, u32[]{:S(2)}) copy-start(s32[2,8]{1,0:T(2,128)} %param.15) | copy-start | bytes 196
  9.5 18.8 %copy-start.4 = (s32[2,8]{1,0:T(2,128)S(1)}, s32[2,8]{1,0:T(2,128)}, u32[]{:S(2)}) copy-start(s32[2,8]{1,0:T(2,128)} %param.14) | copy-start | bytes 196
  9.5 118.9 %all-to-all-start = ((f32[64,2,32,128]{3,2,1,0:T(8,128)}), f32[64,2,32,128]{3,2,1,0:T(8,128)S(1)}, u32[]{:S(2)}, u32[]{:S(2)}) async-start(f32[64,2,32,128]{3,2,1,0:T(8,128)} %stack.4), calls=%async_computation | async-start | bytes 4194304 | tf_op jit(solution)/shard_map/all_to_all | solution.py:35
  131.9 6.0 %copy-start.2 = (s32[2,32]{1,0:T(2,128)S(1)}, s32[2,32]{1,0:T(2,128)}, u32[]{:S(2)}) copy-start(s32[2,32]{1,0:T(2,128)} %param.16) | copy-start | bytes 772
  131.9 6.1 %copy-start.6 = (s32[2,32]{1,0:T(2,128)S(1)}, s32[2,32]{1,0:T(2,128)}, u32[]{:S(2)}) copy-start(s32[2,32]{1,0:T(2,128)} %param.17) | copy-start | bytes 772
  131.9 6.3 %copy-start.5 = (s32[1,64]{1,0:T(1,128)S(1)}, s32[1,64]{1,0:T(1,128)}, u32[]{:S(2)}) copy-start(s32[1,64]{1,0:T(1,128)} %param.13) | copy-start | bytes 772
  131.9 105.7 %all-to-all-start.1 = ((f32[64,2,32,128]{3,2,1,0:T(8,128)}), f32[64,2,32,128]{3,2,1,0:T(8,128)S(1)}, u32[]{:S(2)}, u32[]{:S(2)}) async-start(f32[64,2,32,128]{3,2,1,0:T(8,128)} %stack.5), calls=%async_computation.1 | async-start | bytes 4194304 | tf_op jit(solution)/shard_map/all_to_all | solution.py:35
  237.6 20.4 %all-to-all-start.2 = ((s32[64,1,1]{2,1,0:T(1,128)}), s32[64,1,1]{2,1,0:T(1,128)S(1)}, u32[]{:S(2)}, u32[]{:S(2)}) async-start(s32[64,1,1]{2,1,0:T(1,128)} %copy.50), calls=%async_computation.3 | async-start | bytes 65536 | tf_op jit(solution)/shard_map/all_to_all | solution.py:27
  244.9 0.9 copy-start
  244.9 0.9 copy-start.1
  258.0 61.3 %all-to-all-start.3 = ((f32[64,32,128]{2,1,0:T(8,128)}), f32[64,32,128]{2,1,0:T(8,128)S(1)}, u32[]{:S(2)}, u32[]{:S(2)}) async-start(f32[64,32,128]{2,1,0:T(8,128)} %copy.53), calls=%async_computation.4 | async-start | bytes 2097152 | tf_op jit(solution)/shard_map/all_to_all | solution.py:70
  265.4 40.1 %reduce-scatter.2.cloned.1.call-start = ((), (), s32[]{:S(2)}) async-start(), calls=%async_computation.5 | async-start | bytes 294912 | tf_op jit(solution)/shard_map/reduce_scatter | solution.py:59
Sparse Core Ops, SparseCore 0:
  269.1 36.4 reduce-scatter.1
